TPU v7x, 32 devices: a whole 2x2x4 slice. The times are simulated.
32 devices in a mesh: gx: 8 (over y, x, core), gy: 4 (over z).
Axes of the slice: x: 2, y: 2, z: 4, core: 2. Of those that a mesh axis runs over, the one named last changes fastest.
Arguments:
- diag_blocks: float32 [9, 512, 512], P(None, 'gx', 'gy'), may hold values from 0 to 36, as said below
- edge_blocks: float32 [4, 9, 512, 512], P(None, None, 'gx', 'gy'), may hold values from -0.3 to 0.3
- edge_mask: int32 [4, 512, 512], P(None, 'gx', 'gy'), may hold values 0 or 1
- src_values: float32 [3, 32768], P(None, ('gx', 'gy')), may hold values from -48 to 48
- src_owner: int32 [32768, 1], P(('gx', 'gy')), may hold values from 0 to 7; in each aligned block of 1024 rows (0 to 1023, 1024 to 2047, ...) at most 256 rows name the same one
- src_node: int32 [32768], P(('gx', 'gy')), may hold values from 0 to 8191
- src_count: int32 [32], P(('gx', 'gy')), may hold values from 256 to 1024, as said below
- surf_node: int32 [65536], P(('gx', 'gy')), may hold values from 0 to 8191
- surf_param: float32 [3, 65536], P(None, ('gx', 'gy')), may hold values from 0 to 1
- tile_box: int32 [512], P(('gx', 'gy')), may hold values from 0 to 31
Outputs:
- adjoint_field: float32 [3, 512, 512], P(None, 'gx', 'gy')
- box_gradient: float32 [32, 192], P(('gx', 'gy'))
Inputs may be any that keep to these rules, and one draw needn't show every extreme that they name: `src_owner`: each device's rows name every gx index at most 256 times. `src_count`: some device has all 1024 rows live. `diag_blocks`: entries 0, 4 and 8 lie between 6 and 36; the other entries between 0 and 1.
All inputs are finite; a program needn't handle non-finite values. No bound on the sum of `edge_mask` on one device may be relied on, other than what follows from the above.
Results may differ from a plain program's by a relative error of at most 0.0015.
Values sent between devices are 32-bit elements; how exact they have to be, the bound alone decides.
No kernel may reach another device: no remote copies, remote signals or barrier semaphores. Data moves between devices by JAX's collectives and lax.ppermute only.
A program may use at most 64 MiB of HBM per device.

v0:
```python
import functools

import jax
import jax.numpy as jnp
from jax import lax
from jax.experimental import pallas as pl
from jax.experimental.pallas import tpu as pltpu
from jax.sharding import PartitionSpec as P

F32 = jnp.float32
BF16 = jnp.bfloat16
PAD = 16
NOWHERE = -4096.0
LANES = 128
LOWER = 48
STRIPS = 64
CHUNK = 256
PACK_VMEM = 60 * 1000 * 1000
PARAMS = pltpu.CompilerParams(vmem_limit_bytes=24 * 1024 * 1024)

VMEM = pl.BlockSpec(memory_space=pltpu.VMEM)
SMEM = pl.BlockSpec(memory_space=pltpu.SMEM)
HBM = pl.BlockSpec(memory_space=pltpu.HBM)


def iota(shape, dim):
    return lax.broadcasted_iota(jnp.int32, shape, dim)


def float_iota(shape, dim):
    return iota(shape, dim).astype(F32)


def two_parts(value):
    high = value.astype(BF16).astype(F32)
    return high, value - high


def product(block, field):
    return [
        block(row) * field[0] + block(3 + row) * field[1] + block(6 + row) * field[2]
        for row in range(3)
    ]


def off_diagonal(block, field):
    return [
        sum(block(3 * i + row) * field[i] for i in range(3) if i != row) for row in range(3)
    ]


def masked_product(edge_ref, mask_ref, direction, field):
    mask = mask_ref[direction].astype(F32)
    return [mask * part for part in product(lambda k: edge_ref[direction, k], field)]


def rows_moved(field, edge_row, step):
    size = field.shape[0]
    at = iota(field.shape, 0)
    moved = pltpu.roll(field, step % size, 0)
    return jnp.where(at == (0 if step == 1 else size - 1), edge_row, moved)


def lanes_moved(field, edge_column, step):
    size = field.shape[1]
    at = iota(field.shape, 1)
    moved = pltpu.roll(field, step % size, 1)
    return jnp.where(at == (0 if step == 1 else size - 1), edge_column, moved)


def pack_kernel(
    count_in, values_in, owner_in, node_in, diag_in, edge_in, mask_in, rows_ref,
    count_ref, values_ref, owner_ref, node_ref, diag_low, diag_high, edge_low, edge_high,
    mask_low, mask_high, arrived,
):
    groups = owner_ref.shape[0]
    cells_x = diag_in.shape[1]
    top = pl.ds(cells_x - 8, 8)
    copies = [
        pltpu.make_async_copy(source, target, arrived.at[k])
        for k, (source, target) in enumerate(
            (
                (edge_in.at[1, :, 0:8], edge_low),
                (edge_in.at[:, :, top], edge_high),
                (diag_in.at[:, 0:8], diag_low),
                (diag_in.at[:, top], diag_high),
                (mask_in.at[1, 0:8], mask_low),
                (mask_in.at[:, top], mask_high),
                (values_in, values_ref),
                (owner_in, owner_ref),
                (node_in, node_ref),
                (count_in, count_ref),
            )
        )
    ]
    for copy in copies:
        copy.start()
    statics = 5 * groups
    for copy in copies:
        copy.wait()
    order = iota((groups, LANES), 0) * LANES + iota((groups, LANES), 1)
    node = node_ref[...]
    row = owner_ref[...] * cells_x + lax.shift_right_logical(node, 7)
    row = jnp.where(order < count_ref[0], row.astype(F32), NOWHERE)
    column = (node & (LANES - 1)).astype(F32)
    for comp in range(3):
        for group in range(groups):
            rows_ref[comp * groups + group : comp * groups + group + 1, :] = values_ref[
                comp : comp + 1, group * LANES : (group + 1) * LANES
            ]
    rows_ref[3 * groups : 4 * groups, :] = row
    rows_ref[4 * groups : 5 * groups, :] = column

    def put(slot, value):
        rows_ref[statics + slot : statics + slot + 1, :] = value

    for k in range(9):
        put(k, diag_high[k, 7:8, :])
    for slot, (direction, at) in enumerate(((0, 7), (2, 7), (3, 7), (0, 6))):
        present = mask_high[direction, at : at + 1, :].astype(F32)
        for k in range(9):
            put(9 + 9 * slot + k, edge_high[direction, k, at : at + 1, :] * present)
    for k in range(3):
        put(45 + k, diag_high[4 * k, 6:7, :])
    for k in range(3):
        put(LOWER + k, diag_low[4 * k, 0:1, :])
    present = mask_low[0:1, :].astype(F32)
    for k in range(9):
        put(LOWER + 3 + k, edge_low[k, 0:1, :] * present)
    rows_ref[statics + LOWER + 12 :, :] = jnp.zeros((STRIPS - LOWER - 12, LANES), F32)


def stretched(row, count):
    tile = jnp.broadcast_to(row, (16, row.shape[1])).astype(BF16)
    return jnp.concatenate([tile] * (count // 16), axis=0)


def strip(rows_ref, sender, base, there):
    return lambda first: lambda k: jnp.where(
        there, rows_ref[sender, base + first + k : base + first + k + 1, :], 0.0
    )


def ratio(value, scale):
    return jnp.where(scale > 0.0, value / jnp.where(scale > 0.0, scale, 1.0), 0.0)


def row_before(entry, near, far, entering):
    diag, toward = entry(0), entry(9)
    field = [ratio(near[c], diag(4 * c)) for c in range(3)]
    inverse = [ratio(1.0, diag(4 * c)) for c in range(3)]
    far_field = [ratio(far[c], entry(45)(c)) for c in range(3)]
    into = product(toward, field)
    up_y = product(entry(18), field)
    low_y = product(entry(27), field)
    from_far = product(entry(36), far_field)
    within = off_diagonal(diag, field)
    part = [
        (
            within[c]
            + from_far[c]
            + entering[c]
            + lanes_moved(up_y[c], 0.0, 1)
            + lanes_moved(low_y[c], 0.0, -1)
        )
        * inverse[c]
        for c in range(3)
    ]
    return field, into, part, inverse, up_y, low_y, [toward(k) for k in range(9)]


def field_kernel(
    rows_ref, diag_ref, edge_ref, mask_ref,
    field_ref, part_ref, halo_ref, edges_ref, load_ref,
):
    senders = rows_ref.shape[0]
    groups = (rows_ref.shape[1] - STRIPS) // 5
    cells_x = field_ref.shape[1]
    half = (cells_x + 2 * PAD) // 2
    own = cells_x // 2

    load_ref[...] = jnp.zeros_like(load_ref)
    here = lax.axis_index("gx")
    first_row = (here * cells_x - PAD).astype(F32)

    def add_rows(sender, carry):
        row = rows_ref[sender, 3 * groups : 4 * groups, :] - first_row
        column = rows_ref[sender, 4 * groups : 5 * groups, :]
        lower = row >= float(half)
        place = jnp.where(lower, row - float(half), row)
        column = jnp.where(lower, column + float(LANES), column)
        at_row = float_iota((half, LANES), 0).astype(BF16)
        at_column = float_iota((2 * LANES, LANES), 0).astype(BF16)
        parts = [
            two_parts(rows_ref[sender, c * groups : (c + 1) * groups, :]) for c in range(3)
        ]
        zero, one = jnp.zeros((), BF16), jnp.ones((), BF16)
        lefts, rights = [], []
        for group in range(groups):
            line = slice(group, group + 1)
            match = at_row == stretched(place[line], half)
            lefts.append(
                jnp.concatenate(
                    [
                        jnp.where(match, stretched(parts[c][which][line], half), zero)
                        for which in range(2)
                        for c in range(3)
                    ],
                    axis=0,
                )
            )
            rights.append(
                jnp.where(at_column == stretched(column[line], 2 * LANES), one, zero)
            )
        load_ref[...] += lax.dot_general(
            jnp.concatenate(lefts, axis=1),
            jnp.concatenate(rights, axis=1),
            (((1,), (1,)), ((), ())),
            preferred_element_type=F32,
        )
        return carry

    lax.fori_loop(0, senders, add_rows, 0, unroll=2)

    def load_rows(comp, first, last, second_half):
        lanes = slice(LANES, 2 * LANES) if second_half else slice(0, LANES)
        return (
            load_ref[comp * half + first : comp * half + last, lanes]
            + load_ref[(3 + comp) * half + first : (3 + comp) * half + last, lanes]
        )

    field = []
    for comp in range(3):
        load = jnp.concatenate(
            [load_rows(comp, PAD, half, False), load_rows(comp, 0, half - PAD, True)], axis=0
        )
        field.append(load / diag_ref[4 * comp])
        field_ref[comp] = field[comp]
    beyond = half - PAD
    near_before = [load_rows(c, PAD - 1, PAD, False) for c in range(3)]
    far_before = [load_rows(c, PAD - 2, PAD - 1, False) for c in range(3)]
    near_after = [load_rows(c, beyond, beyond + 1, True) for c in range(3)]

    up_x = masked_product(edge_ref, mask_ref, 0, field)
    low_x = masked_product(edge_ref, mask_ref, 1, field)
    base = 5 * groups
    before = row_before(
        strip(rows_ref, jnp.maximum(here - 1, 0), base, here > 0),
        near_before, far_before, [p[:1] for p in low_x],
    )
    after = strip(
        rows_ref, jnp.minimum(here + 1, senders - 1), base + LOWER, here < senders - 1
    )
    after = product(after(3), [ratio(near_after[c], after(0)(c)) for c in range(3)])
    total = off_diagonal(lambda k: diag_ref[k], field)
    total = [total[c] + rows_moved(up_x[c], before[1][c], 1) for c in range(3)]
    total = [total[c] + rows_moved(low_x[c], after[c], -1) for c in range(3)]
    up_y = masked_product(edge_ref, mask_ref, 2, field)
    low_y = masked_product(edge_ref, mask_ref, 3, field)
    total = [
        total[c] + lanes_moved(up_y[c], 0.0, 1) + lanes_moved(low_y[c], 0.0, -1)
        for c in range(3)
    ]
    inverse = [1.0 / diag_ref[4 * c] for c in range(3)]
    part = [total[c] * inverse[c] for c in range(3)]
    for comp in range(3):
        part_ref[comp] = part[comp]
    for slot, which in enumerate((0, 2, 3)):
        for comp in range(3):
            at = 3 * slot + comp
            halo_ref[at : at + 1, :] = before[which][comp]
    for k in range(9):
        halo_ref[9 + k : 10 + k, :] = before[6][k]
    halo_ref[18:, :] = jnp.zeros((6, LANES), F32)

    def columns(target, lane, along_y, halo_slot):
        ahead = cells_x
        packed = jnp.zeros((cells_x, LANES), F32)
        extra = jnp.zeros((8, LANES), F32)
        at = iota((cells_x, LANES), 1)
        at_extra = iota((8, LANES), 1)
        which_row = iota((8, LANES), 0)
        for slot, fields in enumerate((field, along_y, part, inverse)):
            for comp in range(3):
                column = fields[comp][:, lane : lane + 1]
                packed = jnp.where(at == 3 * slot + comp, column, packed)
        for comp in range(3):
            first = before[halo_slot][comp][:, lane : lane + 1]
            extra = jnp.where((at_extra == 3 + comp) & (which_row == 0), first, extra)
        rest = jnp.zeros((LANES - ahead - 8, LANES), F32)
        whole = jnp.concatenate([packed, extra, rest], axis=0)
        edges_ref[target] = whole.T[:16]

    edges_ref[...] = jnp.zeros_like(edges_ref)
    across = lax.axis_index("gy")

    @pl.when(across < edges_ref.shape[0] - 1)
    def _():
        columns(across + 1, LANES - 1, up_y, 4)

    @pl.when(across > 0)
    def _():
        columns(across - 1, 0, low_y, 5)


def bernstein(coord):
    other = 1.0 - coord
    return [
        other * other * other,
        3.0 * coord * other * other,
        3.0 * coord * coord * other,
        coord * coord * coord,
    ]


def weight_table(u, v, w):
    first, second, third = bernstein(u), bernstein(v), bernstein(w)
    line = iota((8, u.shape[1]), 0)
    inner = line & 3
    along = jnp.where(
        inner == 0,
        third[0],
        jnp.where(inner == 1, third[1], jnp.where(inner == 2, third[2], third[3])),
    )
    pair = jnp.concatenate(
        [
            jnp.where(line < 4, second[0], second[1]) * along,
            jnp.where(line < 4, second[2], second[3]) * along,
        ],
        axis=0,
    )
    return jnp.concatenate([pair * first[i] for i in range(4)], axis=0)


def sums_kernel(
    tile_ref, edges_ref, field_ref, part_ref, halo_ref,
    diag_ref, edge_ref, mask_ref, node_ref, param_ref,
    quotient_ref, out_ref, *, tile_points,
):
    cells_x = field_ref.shape[1]
    own = cells_x // 2
    targets = out_ref.shape[0]

    def arrived(sender):
        rest = jnp.zeros((LANES - 16, LANES), F32)
        return jnp.concatenate([edges_ref[sender], rest], axis=0).T

    across = lax.axis_index("gy")
    low = arrived(jnp.maximum(across - 1, 0))
    high = arrived(jnp.minimum(across + 1, edges_ref.shape[0] - 1))
    lane = iota((cells_x, LANES), 1)

    def column(source, slot, comp):
        return source[:cells_x, 3 * slot + comp : 3 * slot + comp + 1]

    field = [field_ref[c] for c in range(3)]
    scale = [diag_ref[4 * c] for c in range(3)]
    toward_high = masked_product(edge_ref, mask_ref, 2, field)
    toward_low = masked_product(edge_ref, mask_ref, 3, field)
    quotient, low_edge, high_edge = [], [], []
    for c in range(3):
        entering = jnp.where(
            lane == 0,
            column(low, 1, c),
            jnp.where(lane == LANES - 1, column(high, 1, c), 0.0),
        )
        quotient.append(part_ref[c] + entering / scale[c])
        low_edge.append(column(low, 2, c) + column(low, 3, c) * toward_low[c][:, :1])
        high_edge.append(column(high, 2, c) + column(high, 3, c) * toward_high[c][:, -1:])
    for c in range(3):
        quotient_ref[c] = quotient[c]
    lane_row = iota((1, LANES), 1)
    before, before_quotient = [], []
    for c in range(3):
        entering = jnp.where(
            lane_row == 0,
            low[cells_x : cells_x + 1, 3 + c : 4 + c],
            jnp.where(lane_row == LANES - 1, high[cells_x : cells_x + 1, 3 + c : 4 + c], 0.0),
        )
        before.append(halo_ref[c : c + 1, :])
        before_quotient.append(
            halo_ref[3 + c : 4 + c, :] + entering * halo_ref[6 + c : 7 + c, :]
        )

    first_sum = sum(field[c] * scale[c] * field[c] for c in range(3))
    second_sum = sum(field[c] * scale[c] * quotient[c] for c in range(3))
    third_sum = sum(quotient[c] * scale[c] * quotient[c] for c in range(3))
    within = off_diagonal(lambda k: diag_ref[k], quotient)
    fourth_sum = sum(within[c] * field[c] for c in range(3))
    fifth_sum = sum(within[c] * quotient[c] for c in range(3))
    for direction in range(4):
        moving = masked_product(edge_ref, mask_ref, direction, quotient)
        for c in range(3):
            if direction == 0:
                a = rows_moved(field[c], 0.0, -1)
                b = rows_moved(quotient[c], 0.0, -1)
            elif direction == 1:
                a = rows_moved(field[c], before[c], 1)
                b = rows_moved(quotient[c], before_quotient[c], 1)
            elif direction == 2:
                a = lanes_moved(field[c], column(high, 0, c), -1)
                b = lanes_moved(quotient[c], high_edge[c], -1)
            else:
                a = lanes_moved(field[c], column(low, 0, c), 1)
                b = lanes_moved(quotient[c], low_edge[c], 1)
            fourth_sum = fourth_sum + moving[c] * a
            fifth_sum = fifth_sum + moving[c] * b
    incoming = product(lambda k: halo_ref[9 + k : 10 + k, :], before_quotient)
    extra = [0.0, 0.0, 0.0]
    extra.append(sum(incoming[c] * field[c][:1] for c in range(3)))
    extra.append(sum(incoming[c] * quotient[c][:1] for c in range(3)))
    sums = jnp.zeros((1, LANES), F32)
    for k, value in enumerate((first_sum, second_sum, third_sum, fourth_sum, fifth_sum)):
        line = jnp.sum(value, axis=0, keepdims=True) + extra[k]
        sums = jnp.where(lane_row == k, jnp.sum(line, axis=1, keepdims=True), sums)

    order = [field[0], quotient[0], field[2], field[1], quotient[1], quotient[2]]
    folded = [two_parts(jnp.concatenate([f[:own], f[own:]], axis=1)) for f in order]
    table = jnp.concatenate(
        [folded[f][which] for which in range(2) for f in range(6)], axis=0
    ).astype(BF16)
    points = param_ref.shape[1]
    out_ref[...] = jnp.zeros_like(out_ref)
    pieces = CHUNK // LANES
    zero, one = jnp.zeros((), BF16), jnp.ones((), BF16)
    at_node = float_iota((2 * LANES, CHUNK), 0).astype(BF16)
    nothing = jnp.zeros((1, CHUNK), F32)
    first_half = iota((4, LANES), 1) < LANES // 2
    for chunk in range(points // CHUNK):
        node = jnp.concatenate(
            [node_ref[chunk * pieces + k : chunk * pieces + k + 1, :] for k in range(pieces)],
            axis=1,
        )
        row = lax.shift_right_logical(node, 7)
        place = (node & (LANES - 1)) + jnp.where(row >= own, LANES, 0)
        row = jnp.where(row >= own, row - own, row)
        pick = jnp.where(at_node == stretched(place.astype(F32), 2 * LANES), one, zero)
        read = jnp.dot(table, pick, preferred_element_type=F32)
        read = read[: 6 * own] + read[6 * own :]
        here = iota((own, CHUNK), 0) == row
        values = [
            jnp.sum(
                jnp.where(here, read[f * own : (f + 1) * own], 0.0), axis=0, keepdims=True
            )
            for f in range(6)
        ]
        values = two_parts(
            jnp.concatenate(values[:3] + [nothing] + values[3:] + [nothing], axis=0)
        )
        lanes = slice(chunk * CHUNK, (chunk + 1) * CHUNK)
        weights = two_parts(
            weight_table(param_ref[0:1, lanes], param_ref[1:2, lanes], param_ref[2:3, lanes])
        )
        for k in range(CHUNK // tile_points):
            tile = slice(k * tile_points, (k + 1) * tile_points)
            high, low = values[0][:, tile], values[1][:, tile]
            left = jnp.concatenate(
                [
                    jnp.concatenate([high, high], axis=1),
                    jnp.concatenate([low, jnp.zeros_like(low)], axis=1),
                ],
                axis=0,
            ).astype(BF16)
            right = jnp.concatenate([weights[0][:, tile], weights[1][:, tile]], axis=1)
            right = right.astype(BF16)
            term = lax.dot_general(
                left,
                jnp.concatenate([right, right], axis=0),
                (((1,), (1,)), ((), ())),
                preferred_element_type=F32,
            )
            term = term[:8] + term[8:]
            box = tile_ref[chunk * (CHUNK // tile_points) + k]
            out_ref[box] += jnp.where(first_half, term[:4], term[4:])
    for box in range(targets):
        out_ref[box, 3:4, :] = sums


def result_kernel(got_ref, field_ref, quotient_ref, solution_ref, gradient_ref):
    total = jnp.sum(got_ref[...], axis=0)
    rho, a, b, t, u = [total[3:4, k : k + 1] for k in range(5)]
    ratio = a / rho
    norm = rho + a
    step = rho / norm
    rest = jnp.maximum(b - a * ratio, 0.0)
    beta = step * step * rest / rho
    rest_image = (b + u) - ratio * (a + b + a + t) + ratio * ratio * norm
    cross = (a + t) - ratio * norm
    curve = step * step * rest_image - step * beta * (rest + cross) + beta * beta * norm
    second = jnp.where(
        curve > 0.0, step * step * rest / jnp.where(curve > 0.0, curve, 1.0), 0.0
    )
    of_field = step + second * (beta + step * ratio)
    of_quotient = -(step * second)
    for c in range(3):
        solution_ref[c] = of_field * field_ref[c] + of_quotient * quotient_ref[c]
    gradient_ref[:, :LANES] = of_field * total[0:1] + of_quotient * total[1:2]
    gradient_ref[:, LANES:] = (
        of_field * total[2:3, : LANES // 2] + of_quotient * total[2:3, LANES // 2 :]
    )


def per_device(
    diag_blocks, edge_blocks, edge_mask, src_values, src_owner, src_node, src_count,
    surf_node, surf_param, tile_box,
):
    cells_x, cells_y = diag_blocks.shape[1:]
    width_gx, width_gy = lax.axis_size("gx"), lax.axis_size("gy")
    devices = width_gx * width_gy
    groups = src_node.shape[0] // LANES
    whole = functools.partial(jax.ShapeDtypeStruct, dtype=F32)

    cells = 5 * groups + STRIPS
    i32 = jnp.int32
    rows = pl.pallas_call(
        pack_kernel,
        in_specs=[HBM] * 7,
        out_specs=VMEM,
        out_shape=whole((cells, LANES)),
        scratch_shapes=[
            pltpu.SMEM((1,), i32),
            pltpu.VMEM(src_values.shape, F32),
            pltpu.VMEM((groups, LANES), i32),
            pltpu.VMEM((groups, LANES), i32),
            pltpu.VMEM((9, 8, cells_y), F32),
            pltpu.VMEM((9, 8, cells_y), F32),
            pltpu.VMEM((9, 8, cells_y), F32),
            pltpu.VMEM((4, 9, 8, cells_y), F32),
            pltpu.VMEM((8, cells_y), i32),
            pltpu.VMEM((4, 8, cells_y), i32),
            pltpu.SemaphoreType.DMA((10,)),
        ],
        compiler_params=pltpu.CompilerParams(vmem_limit_bytes=PACK_VMEM),
        name="pack_rows_and_edges",
    )(
        src_count, src_values,
        src_owner.reshape(groups, LANES), src_node.reshape(groups, LANES),
        diag_blocks, edge_blocks, edge_mask,
    )
    rows = lax.all_gather(rows, "gx")

    nodes = (3, cells_x, cells_y)
    frame = cells_x + 2 * PAD
    field, part, halo, edges = pl.pallas_call(
        field_kernel,
        in_specs=[VMEM] * 4,
        out_specs=[VMEM] * 4,
        out_shape=[
            whole(nodes), whole(nodes), whole((24, cells_y)), whole((width_gy, 16, LANES)),
        ],
        scratch_shapes=[pltpu.VMEM((3 * frame, 2 * LANES), F32)],
        compiler_params=PARAMS,
        name="load_and_first_product",
    )(rows, diag_blocks, edge_blocks, edge_mask)
    edges = lax.all_to_all(edges, "gy", split_axis=0, concat_axis=0, tiled=True)

    points = surf_node.shape[0]
    quotient, partial = pl.pallas_call(
        functools.partial(sums_kernel, tile_points=points // tile_box.shape[0]),
        in_specs=[SMEM] + [VMEM] * 9,
        out_specs=[VMEM] * 2,
        out_shape=[whole(nodes), whole((devices, 4, LANES))],
        compiler_params=PARAMS,
        name="sums_and_box_parts",
    )(
        tile_box, edges, field, part, halo, diag_blocks, edge_blocks, edge_mask,
        surf_node.reshape(points // LANES, LANES), surf_param,
    )
    got = lax.all_to_all(partial, ("gx", "gy"), split_axis=0, concat_axis=0, tiled=True)
    return pl.pallas_call(
        result_kernel,
        in_specs=[VMEM] * 3,
        out_specs=[VMEM] * 2,
        out_shape=[whole(nodes), whole((1, 192))],
        compiler_params=PARAMS,
        name="steps_and_outputs",
    )(got, field, quotient)


def solution(mesh):
    return jax.shard_map(
        per_device,
        mesh=mesh,
        in_specs=(
            P(None, "gx", "gy"),
            P(None, None, "gx", "gy"),
            P(None, "gx", "gy"),
            P(None, ("gx", "gy")),
            P(("gx", "gy"), None),
            P(("gx", "gy")),
            P(("gx", "gy")),
            P(("gx", "gy")),
            P(None, ("gx", "gy")),
            P(("gx", "gy")),
        ),
        out_specs=(P(None, "gx", "gy"), P(("gx", "gy"), None)),
        check_vma=False,
    )
```

profile of v0, /device:TPU:0, one launch (start us, length us, event | category | flops | bytes accessed | tf_op | source)
XLA Modules:
  0.0 41.0 jit_solution(4018239162199269208)
XLA Ops:
  0.6 0.0 copy-start.2
  0.6 0.0 copy-start
  0.7 0.0 copy-start.1
  1.4 1.7 %pack_rows_and_edges.1 = f32[104,128]{1,0:T(8,128)} custom-call(s32[1]{0:T(128)S(6)} %copy.12.count_in, f32[3,1024]{1,0:T(4,128)} %values_in.1, s32[8,128]{1,0:T(8,128)} %bitcast.6, s32[8,128]{1,0:T(8,128)} %bitcast.7, f32[9,64,128]{2,1,0:T(8,128)} %diag_ref.3, f32[4,9,64,128]{3,2,1,0:T(8,128)} %edge_ref.3, s32[4,64,128]{2,1,0:T(8,128)} %mask_ref.3), custom_call_target="tpu_custom_call" | custom-call | tf_op jit(solution)/shard_map/pack_rows_and_edges/pallas_call | solution.py:515
  3.1 0.0 copy-start.3
  3.1 0.0 copy-start.4
  3.2 0.0 copy-start.5
  3.2 11.4 %all-gather = f32[832,128]{1,0:T(8,128)S(1)} all-gather(f32[104,128]{1,0:T(8,128)} %pack_rows_and_edges.1), channel_id=2, replica_groups=mesh['gx'=8,'gy'=4] {'gx'}, dimensions={0}, use_global_device_ids=true | all-gather | bytes 479232 | tf_op jit(solution)/shard_map/all_gather | solution.py:540
  14.6 0.0 copy-done.2
  14.6 0.0 copy-done
  14.6 0.0 copy-done.1
  14.6 2.5 %load_and_first_product.1 = (f32[3,64,128]{2,1,0:T(8,128)S(1)}, f32[3,64,128]{2,1,0:T(8,128)S(1)}, f32[24,128]{1,0:T(8,128)S(1)}, f32[4,16,128]{2,1,0:T(8,128)S(1)}) custom-call(f32[8,104,128]{2,1,0:T(8,128)S(1)} %bitcast.4, f32[9,64,128]{2,1,0:T(8,128)S(1)} %copy-done.1, f32[4,9,64,128]{3,2,1,0:T(8,128)S(1)} %copy-done, s32[4,64,128]{2,1,0:T(8,128)S(1)} %copy-done.2), custom_call_target="tpu_custom_call" | custom-call | tf_op jit(solution)/shard_map/load_and_first_product/pallas_call | solution.py:544
  17.1 10.3 %all_to_all.10.edges_ref = f32[4,16,128]{2,1,0:T(8,128)S(1)} all-to-all(f32[4,16,128]{2,1,0:T(8,128)S(1)} %get-tuple-element.8), channel_id=1, replica_groups=mesh['gx'=8,'gy'=4] {'gy'}, dimensions={0} | all-to-all | bytes 65536 | tf_op jit(solution)/shard_map/all_to_all | solution.py:555
  27.4 0.0 copy-done.3
  27.4 0.0 copy-done.4
  27.4 0.0 copy-done.5
  27.4 3.2 %sums_and_box_parts.1 = (f32[3,64,128]{2,1,0:T(8,128)S(1)}, f32[32,4,128]{2,1,0:T(4,128)S(1)}) custom-call(s32[16]{0:T(128)S(1)} %copy-done.5, f32[4,16,128]{2,1,0:T(8,128)S(1)} %all_to_all.10.edges_ref, f32[3,64,128]{2,1,0:T(8,128)S(1)} %get-tuple-element.9.field_ref, f32[3,64,128]{2,1,0:T(8,128)S(1)} %get-tuple-element.10.part_ref, ...), custom_call_target="tpu_custom_call" | custom-call | tf_op jit(solution)/shard_map/sums_and_box_parts/pallas_call | solution.py:558
  30.7 9.3 %all_to_all.11.got_ref = f32[32,4,128]{2,1,0:T(4,128)S(1)} all-to-all(f32[32,4,128]{2,1,0:T(4,128)S(1)} %get-tuple-element.12), channel_id=1, replica_groups=mesh['gx'=8,'gy'=4] {'gx','gy'}, dimensions={0} | all-to-all | bytes 131072 | tf_op jit(solution)/shard_map/all_to_all | solution.py:569
  39.9 1.0 %steps_and_outputs.1 = (f32[3,64,128]{2,1,0:T(8,128)}, f32[1,192]{1,0:T(1,128)}) custom-call(f32[32,4,128]{2,1,0:T(4,128)S(1)} %all_to_all.11.got_ref, f32[3,64,128]{2,1,0:T(8,128)S(1)} %get-tuple-element.9.field_ref, f32[3,64,128]{2,1,0:T(8,128)S(1)} %get-tuple-element.13.quotient_ref), custom_call_target="tpu_custom_call" | custom-call | tf_op jit(solution)/shard_map/steps_and_outputs/pallas_call | solution.py:570
Async XLA Ops:
  0.6 14.0 %copy-start.2 = (s32[4,64,128]{2,1,0:T(8,128)S(1)}, s32[4,64,128]{2,1,0:T(8,128)}, u32[]{:S(2)}) copy-start(s32[4,64,128]{2,1,0:T(8,128)} %mask_ref.3) | copy-start | bytes 393220
  0.6 14.0 %copy-start = (f32[4,9,64,128]{3,2,1,0:T(8,128)S(1)}, f32[4,9,64,128]{3,2,1,0:T(8,128)}, u32[]{:S(2)}) copy-start(f32[4,9,64,128]{3,2,1,0:T(8,128)} %edge_ref.3) | copy-start | bytes 3538948
  0.7 14.0 %copy-start.1 = (f32[9,64,128]{2,1,0:T(8,128)S(1)}, f32[9,64,128]{2,1,0:T(8,128)}, u32[]{:S(2)}) copy-start(f32[9,64,128]{2,1,0:T(8,128)} %diag_ref.3) | copy-start | bytes 884740
  3.1 24.3 %copy-start.3 = (f32[3,2048]{1,0:T(4,128)S(1)}, f32[3,2048]{1,0:T(4,128)}, u32[]{:S(2)}) copy-start(f32[3,2048]{1,0:T(4,128)} %param_ref.1) | copy-start | bytes 73732
  3.1 24.3 %copy-start.4 = (s32[2048]{0:T(1024)S(1)}, s32[2048]{0:T(1024)}, u32[]{:S(2)}) copy-start(s32[2048]{0:T(1024)} %param.17) | copy-start | bytes 24580
  3.2 24.3 %copy-start.5 = (s32[16]{0:T(128)S(1)}, s32[16]{0:T(128)}, u32[]{:S(2)}) copy-start(s32[16]{0:T(128)} %tile_ref.1) | copy-start | bytes 196
where the time goes:
time: 41.3 us; the launch traced here: 41 us
  blocking collectives  31 us (75%)
  Pallas kernels  8.42 us (20%)
  between operations  1.47 us (4%)
    all_gather x1, blocking collectives, per_device(): rows = lax.all_gather(rows, 'gx')  11.4 us
    all_to_all x1, blocking collectives, per_device(): edges = lax.all_to_all(edges, 'gy', split_axis=0, concat_axis=0, tiled=True)  10.3 us
    all_to_all x1, blocking collectives, per_device(): lax.all_to_all(partial, ('gx', 'gy'), split_axis=0, concat_axis=0, tiled=...  9.26 us
    pallas_call x1, Pallas kernels, per_device(): pl.pallas_call(functools.partial(sums_kernel, tile_points=points // tile_...  3.23 us
    pallas_call x1, Pallas kernels, per_device(): pl.pallas_call(field_kernel, in_specs=[VMEM] * 4, out_specs=[VMEM] * 4, o...  2.49 us
    pallas_call x1, Pallas kernels, per_device(): pl.pallas_call(pack_kernel, in_specs=[HBM] * 7, out_specs=VMEM, out_shape...  1.7 us
    pallas_call x1, Pallas kernels, per_device(): pl.pallas_call(result_kernel, in_specs=[VMEM] * 3, out_specs=[VMEM] * 2,...  1.01 us

commit v1 on v0

--- a/solution.py
+++ b/solution.py
@@ -171,7 +171,7 @@
 
 def field_kernel(
     rows_ref, diag_ref, edge_ref, mask_ref,
-    field_ref, part_ref, halo_ref, edges_ref, load_ref,
+    field_ref, part_ref, halo_ref, edges_ref, own_ref, load_ref,
 ):
     senders = rows_ref.shape[0]
     groups = (rows_ref.shape[1] - STRIPS) // 5
@@ -220,7 +220,7 @@
         )
         return carry
 
-    lax.fori_loop(0, senders, add_rows, 0, unroll=2)
+    lax.fori_loop(0, senders, add_rows, 0, unroll=min(senders, 8))
 
     def load_rows(comp, first, last, second_half):
         lanes = slice(LANES, 2 * LANES) if second_half else slice(0, LANES)
@@ -273,7 +273,7 @@
         halo_ref[9 + k : 10 + k, :] = before[6][k]
     halo_ref[18:, :] = jnp.zeros((6, LANES), F32)
 
-    def columns(target, lane, along_y, halo_slot):
+    def columns(lane, along_y, halo_slot):
         ahead = cells_x
         packed = jnp.zeros((cells_x, LANES), F32)
         extra = jnp.zeros((8, LANES), F32)
@@ -289,18 +289,22 @@
             extra = jnp.where((at_extra == 3 + comp) & (which_row == 0), first, extra)
         rest = jnp.zeros((LANES - ahead - 8, LANES), F32)
         whole = jnp.concatenate([packed, extra, rest], axis=0)
-        edges_ref[target] = whole.T[:16]
-
+        return whole.T[:16]
+
+    first_column = columns(0, low_y, 5)
+    last_column = columns(LANES - 1, up_y, 4)
+    own_ref[0] = first_column
+    own_ref[1] = last_column
     edges_ref[...] = jnp.zeros_like(edges_ref)
     across = lax.axis_index("gy")
 
     @pl.when(across < edges_ref.shape[0] - 1)
     def _():
-        columns(across + 1, LANES - 1, up_y, 4)
+        edges_ref[across + 1] = last_column
 
     @pl.when(across > 0)
     def _():
-        columns(across - 1, 0, low_y, 5)
+        edges_ref[across - 1] = first_column
 
 
 def bernstein(coord):
@@ -332,13 +336,105 @@
     return jnp.concatenate([pair * first[i] for i in range(4)], axis=0)
 
 
-def sums_kernel(
-    tile_ref, edges_ref, field_ref, part_ref, halo_ref,
-    diag_ref, edge_ref, mask_ref, node_ref, param_ref,
-    quotient_ref, out_ref, *, tile_points,
+def add_tiles(out_ref, tile_ref, high, low, weights):
+    first_half = iota((4, LANES), 1) < LANES // 2
+    tiles = tile_ref.shape[0]
+    points = high.shape[1] // tiles
+    for tile in range(tiles):
+        lanes = slice(tile * points, (tile + 1) * points)
+        one, two = high[:, lanes], low[:, lanes]
+        left = jnp.concatenate(
+            [
+                jnp.concatenate([one, one], axis=1),
+                jnp.concatenate([two, jnp.zeros_like(two)], axis=1),
+            ],
+            axis=0,
+        ).astype(BF16)
+        right = weights(tile)
+        term = lax.dot_general(
+            left,
+            jnp.concatenate([right, right], axis=0),
+            (((1,), (1,)), ((), ())),
+            preferred_element_type=F32,
+        )
+        term = term[:8] + term[8:]
+        out_ref[tile_ref[tile]] += jnp.where(first_half, term[:4], term[4:])
+
+
+def box_kernel(
+    tile_ref, field_ref, part_ref, node_ref, param_ref,
+    box_ref, weights_ref, columns_ref, *, tile_points,
 ):
     cells_x = field_ref.shape[1]
     own = cells_x // 2
+    field = [field_ref[c] for c in range(3)]
+    part = [part_ref[c] for c in range(3)]
+    order = [field[0], part[0], field[2], field[1], part[1], part[2]]
+    folded = [two_parts(jnp.concatenate([f[:own], f[own:]], axis=1)) for f in order]
+    table = jnp.concatenate(
+        [folded[f][which] for which in range(2) for f in range(6)], axis=0
+    ).astype(BF16)
+    points = param_ref.shape[1]
+    pieces = CHUNK // LANES
+    zero, one = jnp.zeros((), BF16), jnp.ones((), BF16)
+    at_node = float_iota((2 * LANES, CHUNK), 0).astype(BF16)
+    nothing = jnp.zeros((1, CHUNK), F32)
+    highs, lows = [], []
+    for chunk in range(points // CHUNK):
+        node = jnp.concatenate(
+            [node_ref[chunk * pieces + k : chunk * pieces + k + 1, :] for k in range(pieces)],
+            axis=1,
+        )
+        row = lax.shift_right_logical(node, 7)
+        column = node & (LANES - 1)
+        lanes = slice(chunk * CHUNK, (chunk + 1) * CHUNK)
+        at_edge = jnp.where(
+            column == 0, row, jnp.where(column == LANES - 1, row + cells_x, -1)
+        ).astype(F32)
+        columns_ref[:, lanes] = jnp.where(
+            at_node[: 2 * cells_x] == stretched(at_edge, 2 * cells_x), one, zero
+        )
+        place = column + jnp.where(row >= own, LANES, 0)
+        row = jnp.where(row >= own, row - own, row)
+        pick = jnp.where(at_node == stretched(place.astype(F32), 2 * LANES), one, zero)
+        read = jnp.dot(table, pick, preferred_element_type=F32)
+        read = read[: 6 * own] + read[6 * own :]
+        here = iota((own, CHUNK), 0) == row
+        values = [
+            jnp.sum(
+                jnp.where(here, read[f * own : (f + 1) * own], 0.0), axis=0, keepdims=True
+            )
+            for f in range(6)
+        ]
+        high, low = two_parts(
+            jnp.concatenate(values[:3] + [nothing] + values[3:] + [nothing], axis=0)
+        )
+        highs.append(high)
+        lows.append(low)
+        weights = two_parts(
+            weight_table(param_ref[0:1, lanes], param_ref[1:2, lanes], param_ref[2:3, lanes])
+        )
+        for k in range(CHUNK // tile_points):
+            tile = slice(k * tile_points, (k + 1) * tile_points)
+            weights_ref[chunk * (CHUNK // tile_points) + k] = jnp.concatenate(
+                [weights[0][:, tile], weights[1][:, tile]], axis=1
+            ).astype(BF16)
+    box_ref[...] = jnp.zeros_like(box_ref)
+    add_tiles(
+        box_ref,
+        tile_ref,
+        jnp.concatenate(highs, axis=1),
+        jnp.concatenate(lows, axis=1),
+        lambda tile: weights_ref[tile],
+    )
+
+
+def sums_kernel(
+    tile_ref, edges_ref, own_ref, field_ref, part_ref, halo_ref,
+    diag_ref, edge_ref, mask_ref, box_ref, weights_ref, columns_ref,
+    quotient_ref, out_ref,
+):
+    cells_x = field_ref.shape[1]
     targets = out_ref.shape[0]
 
     def arrived(sender):
@@ -414,64 +510,24 @@
         line = jnp.sum(value, axis=0, keepdims=True) + extra[k]
         sums = jnp.where(lane_row == k, jnp.sum(line, axis=1, keepdims=True), sums)
 
-    order = [field[0], quotient[0], field[2], field[1], quotient[1], quotient[2]]
-    folded = [two_parts(jnp.concatenate([f[:own], f[own:]], axis=1)) for f in order]
-    table = jnp.concatenate(
-        [folded[f][which] for which in range(2) for f in range(6)], axis=0
-    ).astype(BF16)
-    points = param_ref.shape[1]
-    out_ref[...] = jnp.zeros_like(out_ref)
-    pieces = CHUNK // LANES
-    zero, one = jnp.zeros((), BF16), jnp.ones((), BF16)
-    at_node = float_iota((2 * LANES, CHUNK), 0).astype(BF16)
-    nothing = jnp.zeros((1, CHUNK), F32)
-    first_half = iota((4, LANES), 1) < LANES // 2
-    for chunk in range(points // CHUNK):
-        node = jnp.concatenate(
-            [node_ref[chunk * pieces + k : chunk * pieces + k + 1, :] for k in range(pieces)],
-            axis=1,
-        )
-        row = lax.shift_right_logical(node, 7)
-        place = (node & (LANES - 1)) + jnp.where(row >= own, LANES, 0)
-        row = jnp.where(row >= own, row - own, row)
-        pick = jnp.where(at_node == stretched(place.astype(F32), 2 * LANES), one, zero)
-        read = jnp.dot(table, pick, preferred_element_type=F32)
-        read = read[: 6 * own] + read[6 * own :]
-        here = iota((own, CHUNK), 0) == row
-        values = [
-            jnp.sum(
-                jnp.where(here, read[f * own : (f + 1) * own], 0.0), axis=0, keepdims=True
-            )
-            for f in range(6)
-        ]
-        values = two_parts(
-            jnp.concatenate(values[:3] + [nothing] + values[3:] + [nothing], axis=0)
-        )
-        lanes = slice(chunk * CHUNK, (chunk + 1) * CHUNK)
-        weights = two_parts(
-            weight_table(param_ref[0:1, lanes], param_ref[1:2, lanes], param_ref[2:3, lanes])
-        )
-        for k in range(CHUNK // tile_points):
-            tile = slice(k * tile_points, (k + 1) * tile_points)
-            high, low = values[0][:, tile], values[1][:, tile]
-            left = jnp.concatenate(
-                [
-                    jnp.concatenate([high, high], axis=1),
-                    jnp.concatenate([low, jnp.zeros_like(low)], axis=1),
-                ],
-                axis=0,
-            ).astype(BF16)
-            right = jnp.concatenate([weights[0][:, tile], weights[1][:, tile]], axis=1)
-            right = right.astype(BF16)
-            term = lax.dot_general(
-                left,
-                jnp.concatenate([right, right], axis=0),
-                (((1,), (1,)), ((), ())),
-                preferred_element_type=F32,
-            )
-            term = term[:8] + term[8:]
-            box = tile_ref[chunk * (CHUNK // tile_points) + k]
-            out_ref[box] += jnp.where(first_half, term[:4], term[4:])
+    across_low = edges_ref[jnp.maximum(across - 1, 0)]
+    across_high = edges_ref[jnp.minimum(across + 1, edges_ref.shape[0] - 1)]
+    added = []
+    for c in range(3):
+        first = across_low[3 + c : 4 + c] * own_ref[0, 9 + c : 10 + c, :]
+        second = across_high[3 + c : 4 + c] * own_ref[1, 9 + c : 10 + c, :]
+        added.append(
+            jnp.where(lane_row < cells_x, first, pltpu.roll(second, cells_x, 1))
+        )
+    none = jnp.zeros((1, LANES), F32)
+    added = jnp.concatenate(
+        [none, added[0], none, none, none, added[1], added[2], none], axis=0
+    )
+    added = jnp.concatenate(two_parts(added), axis=0).astype(BF16)
+    read = jnp.dot(added, columns_ref[...], preferred_element_type=F32)
+    high, low = two_parts(read[:8] + read[8:])
+    out_ref[...] = box_ref[...]
+    add_tiles(out_ref, tile_ref, high, low, lambda tile: weights_ref[tile])
     for box in range(targets):
         out_ref[box, 3:4, :] = sums
 
@@ -541,12 +597,13 @@
 
     nodes = (3, cells_x, cells_y)
     frame = cells_x + 2 * PAD
-    field, part, halo, edges = pl.pallas_call(
+    field, part, halo, edges, own = pl.pallas_call(
         field_kernel,
         in_specs=[VMEM] * 4,
-        out_specs=[VMEM] * 4,
+        out_specs=[VMEM] * 5,
         out_shape=[
             whole(nodes), whole(nodes), whole((24, cells_y)), whole((width_gy, 16, LANES)),
+            whole((2, 16, LANES)),
         ],
         scratch_shapes=[pltpu.VMEM((3 * frame, 2 * LANES), F32)],
         compiler_params=PARAMS,
@@ -554,17 +611,34 @@
     )(rows, diag_blocks, edge_blocks, edge_mask)
     edges = lax.all_to_all(edges, "gy", split_axis=0, concat_axis=0, tiled=True)
 
-    points = surf_node.shape[0]
+    points, tiles = surf_node.shape[0], tile_box.shape[0]
+    boxes = (devices, 4, LANES)
+    box_part, weights, columns = pl.pallas_call(
+        functools.partial(box_kernel, tile_points=points // tiles),
+        in_specs=[SMEM] + [VMEM] * 4,
+        out_specs=[VMEM] * 3,
+        out_shape=[
+            whole(boxes),
+            jax.ShapeDtypeStruct((tiles, 64, 2 * points // tiles), BF16),
+            jax.ShapeDtypeStruct((2 * cells_x, points), BF16),
+        ],
+        compiler_params=PARAMS,
+        cost_estimate=pl.CostEstimate(
+            flops=10**9, bytes_accessed=4 * 10**6, transcendentals=0
+        ),
+        name="box_parts",
+    )(tile_box, field, part, surf_node.reshape(points // LANES, LANES), surf_param)
+
     quotient, partial = pl.pallas_call(
-        functools.partial(sums_kernel, tile_points=points // tile_box.shape[0]),
-        in_specs=[SMEM] + [VMEM] * 9,
+        sums_kernel,
+        in_specs=[SMEM] + [VMEM] * 11,
         out_specs=[VMEM] * 2,
-        out_shape=[whole(nodes), whole((devices, 4, LANES))],
+        out_shape=[whole(nodes), whole(boxes)],
         compiler_params=PARAMS,
-        name="sums_and_box_parts",
+        name="sums_and_halo_parts",
     )(
-        tile_box, edges, field, part, halo, diag_blocks, edge_blocks, edge_mask,
-        surf_node.reshape(points // LANES, LANES), surf_param,
+        tile_box, edges, own, field, part, halo, diag_blocks, edge_blocks, edge_mask,
+        box_part, weights, columns,
     )
     got = lax.all_to_all(partial, ("gx", "gy"), split_axis=0, concat_axis=0, tiled=True)
     return pl.pallas_call(

time: 41.3 us -> 39.9 us (0.966)
  blocking collectives: 31 us -> 20.7 us
  starting transfers between devices: 0 us -> 4.88 us
  waiting for transfers between devices: 0 us -> 4.23 us
    all_to_all x1 -> x0, blocking collectives: 10.3 us -> none  [per_device(): edges = lax.all_to_all(edges, 'gy', split_axis=0, concat_axis=0, tiled=True)]
    all_to_all x0 -> x1, starting transfers between devices: none -> 4.88 us  [per_device(): edges = lax.all_to_all(edges, 'gy', split_axis=0, concat_axis=0, tiled=True)]
    all_to_all x0 -> x1, waiting for transfers between devices: none -> 4.23 us  [per_device(): edges = lax.all_to_all(edges, 'gy', split_axis=0, concat_axis=0, tiled=True)]
    pallas_call x2 -> x3, Pallas kernels: 5.72 us -> 5.52 us  [the longest x1 2.52 us: per_device(): pl.pallas_call(field_kernel, in_specs=[VMEM] * 4, out_specs=[VMEM] * 5, o...]
  transfers between devices with their start and end apart: 0 -> 1, of which waited for: 0 -> 1; matrix products, arithmetic and copies ran while one was open for 0% -> 0% of each run, Pallas kernels for 0% -> 4%
where the time goes in v1:
time: 39.9 us; the launch traced here: 39.5 us
  blocking collectives  20.7 us (52%)
  Pallas kernels  8.23 us (21%)
  starting transfers between devices  4.88 us (12%)
  waiting for transfers between devices  4.23 us (11%)
  between operations  1.47 us (4%)
    all_gather x1, blocking collectives, per_device(): rows = lax.all_gather(rows, 'gx')  11.4 us
    all_to_all x1, blocking collectives, per_device(): lax.all_to_all(partial, ('gx', 'gy'), split_axis=0, concat_axis=0, tiled=...  9.27 us
    all_to_all x1, starting transfers between devices, per_device(): edges = lax.all_to_all(edges, 'gy', split_axis=0, concat_axis=0, tiled=True)  4.88 us
    all_to_all x1, waiting for transfers between devices, per_device(): edges = lax.all_to_all(edges, 'gy', split_axis=0, concat_axis=0, tiled=True)  4.23 us
    pallas_call x1, Pallas kernels, per_device(): pl.pallas_call(field_kernel, in_specs=[VMEM] * 4, out_specs=[VMEM] * 5, o...  2.52 us
    pallas_call x1, Pallas kernels, per_device(): pl.pallas_call(pack_kernel, in_specs=[HBM] * 7, out_specs=VMEM, out_shape...  1.7 us
    pallas_call x1, Pallas kernels, per_device(): pl.pallas_call(sums_kernel, in_specs=[SMEM] + [VMEM] * 11, out_specs=[VME...  1.59 us
    pallas_call x1, Pallas kernels, per_device(): pl.pallas_call(functools.partial(box_kernel, tile_points=points // tiles)...  1.41 us
  transfers between devices with their start and end apart: 1, of which 1 were waited for; matrix products, arithmetic and copies ran while one was open for 0% of the time, Pallas kernels for 4%

profile of v1, /device:TPU:0, one launch (start us, length us, event | category | flops | bytes accessed | tf_op | source)
XLA Modules:
  0.0 39.5 jit_solution(15305017625979021129)
XLA Ops:
  0.6 0.0 copy-start.2
  0.6 0.0 copy-start
  0.7 0.0 copy-start.1
  1.4 1.7 %pack_rows_and_edges.1 = f32[104,128]{1,0:T(8,128)} custom-call(s32[1]{0:T(128)S(6)} %copy.12.count_in, f32[3,1024]{1,0:T(4,128)} %values_in.1, s32[8,128]{1,0:T(8,128)} %bitcast.6, s32[8,128]{1,0:T(8,128)} %bitcast.7, f32[9,64,128]{2,1,0:T(8,128)} %diag_ref.3, f32[4,9,64,128]{3,2,1,0:T(8,128)} %edge_ref.3, s32[4,64,128]{2,1,0:T(8,128)} %mask_ref.3), custom_call_target="tpu_custom_call" | custom-call | tf_op jit(solution)/shard_map/pack_rows_and_edges/pallas_call | solution.py:571
  3.1 0.0 copy-start.3
  3.1 0.0 copy-start.4
  3.2 0.0 copy-start.5
  3.2 11.4 %all-gather = f32[832,128]{1,0:T(8,128)S(1)} all-gather(f32[104,128]{1,0:T(8,128)} %pack_rows_and_edges.1), channel_id=2, replica_groups=mesh['gx'=8,'gy'=4] {'gx'}, dimensions={0}, use_global_device_ids=true | all-gather | bytes 479232 | tf_op jit(solution)/shard_map/all_gather | solution.py:596
  14.6 0.0 copy-done.2
  14.6 0.0 copy-done
  14.6 0.0 copy-done.1
  14.6 2.5 %load_and_first_product.1 = (f32[3,64,128]{2,1,0:T(8,128)S(1)}, f32[3,64,128]{2,1,0:T(8,128)S(1)}, f32[24,128]{1,0:T(8,128)S(1)}, f32[4,16,128]{2,1,0:T(8,128)}, f32[2,16,128]{2,1,0:T(8,128)S(1)}) custom-call(f32[8,104,128]{2,1,0:T(8,128)S(1)} %bitcast.4, f32[9,64,128]{2,1,0:T(8,128)S(1)} %copy-done.1, f32[4,9,64,128]{3,2,1,0:T(8,128)S(1)} %copy-done, ...), custom_call_target="tpu_custom_call" | custom-call | tf_op jit(solution)/shard_map/load_and_first_product/pallas_call | solution.py:600
  17.1 4.9 %all-to-all-start = ((f32[4,16,128]{2,1,0:T(8,128)}), f32[4,16,128]{2,1,0:T(8,128)S(1)}, u32[]{:S(2)}, u32[]{:S(2)}) async-start(f32[4,16,128]{2,1,0:T(8,128)} %get-tuple-element.12), calls=%async_computation | async-start | bytes 65536 | tf_op jit(solution)/shard_map/all_to_all | solution.py:612
  22.0 0.0 copy-done.3
  22.0 0.0 copy-done.4
  22.0 0.0 copy-done.5
  22.0 1.4 %box_parts.1 = (f32[32,4,128]{2,1,0:T(4,128)S(1)}, bf16[16,64,256]{2,1,0:T(8,128)(2,1)S(1)}, bf16[128,2048]{1,0:T(8,128)(2,1)S(1)}) custom-call(s32[16]{0:T(128)S(1)} %copy-done.3, f32[3,64,128]{2,1,0:T(8,128)S(1)} %get-tuple-element.14.field_ref, f32[3,64,128]{2,1,0:T(8,128)S(1)} %get-tuple-element.15.part_ref, s32[16,128]{1,0:T(8,128)S(1)} %bitcast.5, ...), custom_call_target="tpu_custom_call" | custom-call | flops 1000000000 | bytes 4000000 | tf_op jit(solution)/shard_map/box_parts/pallas_call | solution.py:616
  23.4 4.2 %all-to-all-done.edges_ref = f32[4,16,128]{2,1,0:T(8,128)S(1)} async-done(((f32[4,16,128]{2,1,0:T(8,128)}), f32[4,16,128]{2,1,0:T(8,128)S(1)}, u32[]{:S(2)}, u32[]{:S(2)}) %all-to-all-start) | async-done | bytes 32800 | tf_op jit(solution)/shard_map/all_to_all | solution.py:612
  27.7 1.6 %sums_and_halo_parts.1 = (f32[3,64,128]{2,1,0:T(8,128)S(1)}, f32[32,4,128]{2,1,0:T(4,128)S(1)}) custom-call(s32[16]{0:T(128)S(1)} %copy-done.3, f32[4,16,128]{2,1,0:T(8,128)S(1)} %all-to-all-done.edges_ref, f32[2,16,128]{2,1,0:T(8,128)S(1)} %get-tuple-element.13.own_ref, f32[3,64,128]{2,1,0:T(8,128)S(1)} %get-tuple-element.14.field_ref, ...), custom_call_target="tpu_custom_call" | custom-call | tf_op jit(solution)/shard_map/sums_and_halo_parts/pallas_call | solution.py:632
  29.3 9.3 %all_to_all.10.got_ref = f32[32,4,128]{2,1,0:T(4,128)S(1)} all-to-all(f32[32,4,128]{2,1,0:T(4,128)S(1)} %get-tuple-element.20), channel_id=1, replica_groups=mesh['gx'=8,'gy'=4] {'gx','gy'}, dimensions={0} | all-to-all | bytes 131072 | tf_op jit(solution)/shard_map/all_to_all | solution.py:643
  38.5 1.0 %steps_and_outputs.1 = (f32[3,64,128]{2,1,0:T(8,128)}, f32[1,192]{1,0:T(1,128)}) custom-call(f32[32,4,128]{2,1,0:T(4,128)S(1)} %all_to_all.10.got_ref, f32[3,64,128]{2,1,0:T(8,128)S(1)} %get-tuple-element.14.field_ref, f32[3,64,128]{2,1,0:T(8,128)S(1)} %get-tuple-element.21.quotient_ref), custom_call_target="tpu_custom_call" | custom-call | tf_op jit(solution)/shard_map/steps_and_outputs/pallas_call | solution.py:644
Async XLA Ops:
  0.6 14.0 %copy-start.2 = (s32[4,64,128]{2,1,0:T(8,128)S(1)}, s32[4,64,128]{2,1,0:T(8,128)}, u32[]{:S(2)}) copy-start(s32[4,64,128]{2,1,0:T(8,128)} %mask_ref.3) | copy-start | bytes 393220
  0.6 14.0 %copy-start = (f32[4,9,64,128]{3,2,1,0:T(8,128)S(1)}, f32[4,9,64,128]{3,2,1,0:T(8,128)}, u32[]{:S(2)}) copy-start(f32[4,9,64,128]{3,2,1,0:T(8,128)} %edge_ref.3) | copy-start | bytes 3538948
  0.7 14.0 %copy-start.1 = (f32[9,64,128]{2,1,0:T(8,128)S(1)}, f32[9,64,128]{2,1,0:T(8,128)}, u32[]{:S(2)}) copy-start(f32[9,64,128]{2,1,0:T(8,128)} %diag_ref.3) | copy-start | bytes 884740
  3.1 18.9 %copy-start.3 = (s32[16]{0:T(128)S(1)}, s32[16]{0:T(128)}, u32[]{:S(2)}) copy-start(s32[16]{0:T(128)} %tile_ref.3) | copy-start | bytes 196
  3.1 18.9 %copy-start.4 = (f32[3,2048]{1,0:T(4,128)S(1)}, f32[3,2048]{1,0:T(4,128)}, u32[]{:S(2)}) copy-start(f32[3,2048]{1,0:T(4,128)} %param_ref.1) | copy-start | bytes 73732
  3.2 18.9 %copy-start.5 = (s32[2048]{0:T(1024)S(1)}, s32[2048]{0:T(1024)}, u32[]{:S(2)}) copy-start(s32[2048]{0:T(1024)} %param.17) | copy-start | bytes 24580
  17.1 10.5 %all-to-all-start = ((f32[4,16,128]{2,1,0:T(8,128)}), f32[4,16,128]{2,1,0:T(8,128)S(1)}, u32[]{:S(2)}, u32[]{:S(2)}) async-start(f32[4,16,128]{2,1,0:T(8,128)} %get-tuple-element.12), calls=%async_computation | async-start | bytes 65536 | tf_op jit(solution)/shard_map/all_to_all | solution.py:612
